TPU v7x, 32 devices: a whole 2x2x4 slice. The times are simulated.
32 devices in a mesh: lon: 8 (over y, x, core), lat: 4 (over z).
Axes of the slice: x: 2, y: 2, z: 4, core: 2. Of those that a mesh axis runs over, the one named last changes fastest.
Arguments:
- cotangent: float32 [4, 1, 1024, 2048], P(None, None, 'lat', 'lon'), may hold values from -6 to 6
- lat_cell: int32 [1, 1024, 2048], P(None, 'lat', 'lon'), may hold values from 0 to 1023, as said below
- lat_frac: float32 [1, 1024, 2048], P(None, 'lat', 'lon'), may hold values from 0 to 1, as said below
- lat_end_cell: int32 [1, 4, 2048], P(None, 'lat', 'lon'), may hold values from 0 to 1023, as said below
- lat_end_frac: float32 [1, 4, 2048], P(None, 'lat', 'lon'), may hold values from 0 to 1, as said below
- lon_cell: int32 [1, 1024, 2048], P(None, 'lat', 'lon'), may hold values from 0 to 2047, as said below
- lon_frac: float32 [1, 1024, 2048], P(None, 'lat', 'lon'), may hold values from 0 to 1, as said below
- lon_end_cell: int32 [1, 1024, 8], P(None, 'lat', 'lon'), may hold values from 0 to 2047, as said below
- lon_end_frac: float32 [1, 1024, 8], P(None, 'lat', 'lon'), may hold values from 0 to 1, as said below
Outputs:
- mass_grad: float32 [4, 1, 1024, 2048], P(None, None, 'lat', 'lon')
Inputs may be any that keep to these rules, and one draw needn't show every extreme that they name: lat_cell + lat_frac never falls along latitude and lies strictly between n - 32 and n + 32 for arrival row n (within the grid); row 0 has edge 0. `lat_frac`: holds the fractional part of the edges of lat_cell; an edge on a cell boundary is given as the lower cell with 1. `lat_end_cell`: the end edge of block b equals the left edge of row (256 * (b + 1)), given as the lower cell with 1 on a boundary; the last block's is 1023 with fraction 1. `lat_end_frac`: fractional parts of the end edges. lon_cell + lon_frac never falls along longitude and lies in (n - 256, n] for arrival column n (upstream only); column 0 has edge 0. `lon_frac`: holds the fractional part of the edges of lon_cell; an edge on a cell boundary is given as the lower cell with 1. `lon_end_cell`: the end edge of block b equals the left edge of column (256 * (b + 1)), given as the lower cell with 1 on a boundary; the last block's is 2047 with fraction 1. `lon_end_frac`: fractional parts of the end edges.
All inputs are finite; a program needn't handle non-finite values.
Results may differ from a plain program's by a relative error of at most 0.0003.
Values sent between devices are 32-bit elements; how exact they have to be, the bound alone decides.
A program may use at most 64 MiB of HBM per device.

v0:
```python
import functools

import jax
import jax.numpy as jnp
from jax import lax
from jax.experimental import pallas as pl
from jax.experimental.pallas import tpu as pltpu
from jax.sharding import PartitionSpec as P

REACH = 32
GROUP = 64


def take(table, at):
    return jnp.take_along_axis(table, at, axis=1, mode="promise_in_bounds")


def lanes_of(rows, half):
    return lax.broadcasted_iota(jnp.int32, (rows, half), 1)


def upper(length):
    before = lax.broadcasted_iota(jnp.int32, (length, length), 0)
    after = lax.broadcasted_iota(jnp.int32, (length, length), 1)
    return jnp.where(before < after, 1.0, 0.0).astype(jnp.bfloat16)


def running(edges, end, values, tri):
    rows, half = edges[0].shape
    lane = lanes_of(rows, half)
    back = [pltpu.roll(edge, half - 1, 1) for edge in edges]
    width = [
        jnp.where(lane == half - 1, back[1], back[0]) - edges[0],
        jnp.where(lane == half - 1, end, back[1]) - edges[1],
    ]
    whole = jnp.concatenate(
        [jnp.concatenate([v[0] * width[0], v[1] * width[1]], axis=1) for v in values], axis=0
    )
    high = whole.astype(jnp.bfloat16)
    low = (whole - high.astype(jnp.float32)).astype(jnp.bfloat16)
    total = jnp.dot(high, tri, preferred_element_type=jnp.float32) + jnp.dot(
        low, tri, preferred_element_type=jnp.float32
    )
    return [
        (total[t * rows : (t + 1) * rows, :half], total[t * rows : (t + 1) * rows, half:])
        for t in range(len(values))
    ]


def integral(points, halves, edges, end, values, sums):
    rows, half = edges[0].shape
    first = jnp.broadcast_to(edges[0][:, :1], (rows, half))
    x = jnp.minimum(jnp.maximum(points, first), end)
    if len(halves) == 2:
        upper_half = jnp.broadcast_to(edges[1][:, :1], (rows, half)) <= x

    def fetch(pair, at):
        if len(halves) == 1:
            return take(pair[halves[0]], at)
        return jnp.where(upper_half, take(pair[1], at), take(pair[0], at))

    at = jnp.zeros((rows, half), jnp.int32)
    step = half // 2
    while step:
        further = at + step
        at = jnp.where(fetch(edges, further) <= x, further, at)
        step //= 2
    inside = x - fetch(edges, at)
    return [fetch(s, at) + fetch(v, at) * inside for s, v in zip(sums, values)]


def step_up(now, before):
    lane = lanes_of(*now.shape)
    return now - jnp.where(lane == 0, before if before is None else pltpu.roll(before, 1, 1), pltpu.roll(now, 1, 1))


def lat_kernel(cot_ref, cell_ref, frac_ref, endc_ref, endf_ref, own_ref, halo_ref, vt, et, endt, mt):
    tracers, lat_rows, cols = cot_ref.shape
    half = lat_rows // 2
    first_cell = lax.axis_index("lat") * lat_rows
    edges = (cell_ref[...] - first_cell).astype(jnp.float32) + frac_ref[...]
    et[...] = edges.T
    end = (endc_ref[...] - first_cell).astype(jnp.float32) + endf_ref[...]
    endt[...] = jnp.broadcast_to(end, (half, cols)).T
    for t in range(tracers):
        vt[t] = cot_ref[t].T
    tri = upper(lat_rows)
    group = min(GROUP, cols)

    @pl.loop(0, cols // group)
    def _(g):
        at = pl.ds(pl.multiple_of(g * group, group), group)
        pair = (et[at, :half], et[at, half:])
        last = endt[at, :]
        values = [(vt[t, at, :half], vt[t, at, half:]) for t in range(tracers)]
        sums = running(pair, last, values, tri)
        lane = lanes_of(group, half)
        places = (
            jnp.where(lane < half // 2, lane + 2 * half, lane - half),
            lane,
            lane + half,
        )
        got = [
            integral((p + 1).astype(jnp.float32), (0, 1), pair, last, values, sums)
            for p in places
        ]
        for t in range(tracers):
            for b in range(3):
                mt[t, b, at, :] = step_up(got[b][t], got[b - 1][t])

    for t in range(tracers):
        halo_ref[t] = mt[t, 0].T
        own_ref[t, :half] = mt[t, 1].T
        own_ref[t, half:] = mt[t, 2].T


def lon_kernel(mid_ref, cell_ref, frac_ref, endc_ref, endf_ref, own_ref, low_ref):
    tracers, rows, cols = mid_ref.shape
    half = cols // 2
    first_cell = lax.axis_index("lon") * cols
    tri = upper(cols)
    group = min(GROUP, rows)

    @pl.loop(0, rows // group)
    def _(g):
        at = pl.ds(pl.multiple_of(g * group, group), group)
        edges = (cell_ref[at, :] - first_cell).astype(jnp.float32) + frac_ref[at, :]
        pair = (edges[:, :half], edges[:, half:])
        last = (endc_ref[at, :] - first_cell).astype(jnp.float32) + endf_ref[at, :]
        last = jnp.broadcast_to(last, (group, half))
        values = [(mid_ref[t, at, :half], mid_ref[t, at, half:]) for t in range(tracers)]
        sums = running(pair, last, values, tri)
        lane = lanes_of(group, half)
        halves = ((0,), (0, 1), (0, 1), (1,))
        got = [
            integral((lane + ((b - 2) * half + 1)).astype(jnp.float32), halves[b], pair, last, values, sums)
            for b in range(4)
        ]
        none = jnp.zeros((group, half), jnp.float32)
        for t in range(tracers):
            for b in range(4):
                target = low_ref if b < 2 else own_ref
                start = (b % 2) * half
                target[t, at, start : start + half] = step_up(
                    got[b][t], got[b - 1][t] if b else none
                )


def passed_along(shard, axis, by):
    count = lax.axis_size(axis)
    pairs = [(i, i + by) for i in range(count) if 0 <= i + by < count]
    return lax.ppermute(shard, axis, pairs)


def shards(cotangent, lat_cell, lat_frac, lat_end_cell, lat_end_frac, lon_cell, lon_frac, lon_end_cell, lon_end_frac):
    tracers, levels, rows, cols = cotangent.shape
    f32 = jnp.float32
    half = rows // 2
    own, halo = pl.pallas_call(
        lat_kernel,
        out_shape=(
            jax.ShapeDtypeStruct((tracers, rows, cols), f32),
            jax.ShapeDtypeStruct((tracers, half, cols), f32),
        ),
        scratch_shapes=[
            pltpu.VMEM((tracers, cols, rows), f32),
            pltpu.VMEM((cols, rows), f32),
            pltpu.VMEM((cols, half), f32),
            pltpu.VMEM((tracers, 3, cols, half), f32),
        ],
        compiler_params=pltpu.CompilerParams(vmem_limit_bytes=48 * 2**20),
        name="lat_pass",
    )(
        cotangent.reshape(tracers, rows, cols),
        lat_cell.reshape(rows, cols),
        lat_frac.reshape(rows, cols),
        lat_end_cell.reshape(1, cols),
        lat_end_frac.reshape(1, cols),
    )
    from_low = passed_along(halo[:, :REACH], "lat", 1)
    from_high = passed_along(halo[:, half - REACH :], "lat", -1)
    middle = own.at[:, :REACH].add(from_low).at[:, rows - REACH :].add(from_high)
    own_part, low_part = pl.pallas_call(
        lon_kernel,
        out_shape=(
            jax.ShapeDtypeStruct((tracers, rows, cols), f32),
            jax.ShapeDtypeStruct((tracers, rows, cols), f32),
        ),
        compiler_params=pltpu.CompilerParams(vmem_limit_bytes=48 * 2**20),
        name="lon_pass",
    )(
        middle,
        lon_cell.reshape(rows, cols),
        lon_frac.reshape(rows, cols),
        lon_end_cell.reshape(rows, 1),
        lon_end_frac.reshape(rows, 1),
    )
    out = own_part + passed_along(low_part, "lon", -1)
    return out.reshape(cotangent.shape)


def solution(mesh):
    whole = P(None, None, "lat", "lon")
    placed = (whole,) + (P(None, "lat", "lon"),) * 8
    return jax.shard_map(shards, mesh=mesh, in_specs=placed, out_specs=whole, check_vma=False)
```

profile of v0, /device:TPU:1, one launch (start us, length us, event | category | flops | bytes accessed | tf_op | source)
XLA Modules:
  0.0 57.0 jit_solution(14293927067624697429)
XLA Ops:
  0.0 0.7 %copy-done.6 = f32[1,1,256]{2,1,0:T(1,128)S(1)} copy-done((f32[1,1,256]{2,1,0:T(1,128)S(1)}, f32[1,1,256]{2,1,0:T(1,128)}, u32[]{:S(2)}) %copy-start.6) | copy-done | bytes 1048
  0.7 0.0 copy-done.5
  0.7 1.2 %copy-done = f32[4,1,256,256]{3,2,1,0:T(8,128)S(1)} copy-done((f32[4,1,256,256]{3,2,1,0:T(8,128)S(1)}, f32[4,1,256,256]{3,2,1,0:T(8,128)}, u32[]{:S(2)}) %copy-start) | copy-done | bytes 1048600
  1.9 0.9 %copy-done.3 = s32[1,256,256]{2,1,0:T(8,128)S(1)} copy-done((s32[1,256,256]{2,1,0:T(8,128)S(1)}, s32[1,256,256]{2,1,0:T(8,128)}, u32[]{:S(2)}) %copy-start.3) | copy-done | bytes 262168
  2.9 0.9 %copy-done.4 = f32[1,256,256]{2,1,0:T(8,128)S(1)} copy-done((f32[1,256,256]{2,1,0:T(8,128)S(1)}, f32[1,256,256]{2,1,0:T(8,128)}, u32[]{:S(2)}) %copy-start.4) | copy-done | bytes 262168
  3.8 12.0 %lat_pass.1 = (f32[4,256,256]{2,1,0:T(8,128)S(1)}, f32[4,128,256]{2,1,0:T(8,128)S(1)}) custom-call(f32[4,256,256]{2,1,0:T(8,128)S(1)} %bitcast.13, s32[256,256]{1,0:T(8,128)S(1)} %bitcast.16, f32[256,256]{1,0:T(8,128)S(1)} %bitcast.17, s32[1,256]{1,0:T(1,128)S(1)} %bitcast.18, f32[1,256]{1,0:T(1,128)S(1)} %bitcast.19), custom_call_target="tpu_custom_call" | custom-call | tf_op jit(solution)/shard_map/lat_pass/pallas_call | solution.py:159
  15.8 4.0 %collective-permute-start = (f32[4,32,256]{2,1,0:T(8,128)S(1)}, f32[4,32,256]{2,1,0:T(8,128)S(1)}, u32[]{:S(2)}, u32[]{:S(2)}) collective-permute-start(f32[4,32,256]{2,1,0:T(8,128)S(1)} %get-tuple-element.38), channel_id=1, source_target_pairs={{0,1},{1,2},{2,3},{4,5},{5,6},{6,7},{8,9},{9,10},{10,11},{12,13},{... | collective-permute-start | bytes 393224 | tf_op jit(solution)/shard_map/ppermute | solution.py:152
  19.9 0.0 copy-start.7
  19.9 1.3 %collective-permute-start.1 = (f32[4,32,256]{2,1,0:T(8,128)S(1)}, f32[4,32,256]{2,1,0:T(8,128)S(1)}, u32[]{:S(2)}, u32[]{:S(2)}) collective-permute-start(f32[4,32,256]{2,1,0:T(8,128)S(1)} %get-tuple-element.37), channel_id=1, source_target_pairs={{1,0},{2,1},{3,2},{5,4},{6,5},{7,6},{9,8},{10,9},{11,10},{13,12},{... | collective-permute-start | bytes 393224 | tf_op jit(solution)/shard_map/ppermute | solution.py:152
  21.2 0.0 copy-done.7
  21.2 0.1 copy.11.endc_ref
  21.3 0.0 copy-start.8
  21.3 0.7 %copy-done.8 = f32[1,256,1]{1,2,0:T(1,128)S(1)} copy-done((f32[1,256,1]{1,2,0:T(1,128)S(1)}, f32[1,256,1]{1,2,0:T(1,128)}, u32[]{:S(2)}) %copy-start.8) | copy-done | bytes 1048
  22.0 0.1 copy.12.endf_ref
  22.1 0.0 collective-permute-done
  22.2 0.0 copy-start.2
  22.2 0.0 copy-start.1
  22.2 3.4 %collective-permute-done.1 = f32[4,32,256]{2,1,0:T(8,128)S(1)} collective-permute-done((f32[4,32,256]{2,1,0:T(8,128)S(1)}, f32[4,32,256]{2,1,0:T(8,128)S(1)}, u32[]{:S(2)}, u32[]{:S(2)}) %collective-permute-start.1) | collective-permute-done | bytes 131104 | tf_op jit(solution)/shard_map/ppermute | solution.py:152
  25.6 0.0 copy-done.2
  25.6 0.0 copy-done.1
  25.6 12.7 %lon_pass.1 = (f32[4,256,256]{2,1,0:T(8,128)S(1)}, f32[4,256,256]{2,1,0:T(8,128)S(1)}) custom-call(f32[4,256,256]{2,1,0:T(8,128)S(1)} %fusion.mid_ref, s32[256,256]{1,0:T(8,128)S(1)} %bitcast.14, f32[256,256]{1,0:T(8,128)S(1)} %bitcast.15, s32[256,1]{1,0:T(8,128)S(1)} %copy.11.endc_ref, f32[256,1]{1,0:T(8,128)S(1)} %copy.12.endf_ref), custom_call_target="tpu_custom_call" | custom-call | tf_op jit(solution)/shard_map/lon_pass/pallas_call | solution.py:183
  38.3 4.0 %collective-permute-start.2 = (f32[4,256,256]{2,1,0:T(8,128)S(1)}, f32[4,256,256]{2,1,0:T(8,128)S(1)}, u32[]{:S(2)}, u32[]{:S(2)}) collective-permute-start(f32[4,256,256]{2,1,0:T(8,128)S(1)} %get-tuple-element.36), channel_id=1, source_target_pairs={{4,0},{8,4},{12,8},{16,12},{20,16},{24,20},{28,24},{5,1},{9,5},{13... | collective-permute-start | bytes 3145736 | tf_op jit(solution)/shard_map/ppermute | solution.py:152
  42.3 13.6 %collective-permute-done.2 = f32[4,256,256]{2,1,0:T(8,128)S(1)} collective-permute-done((f32[4,256,256]{2,1,0:T(8,128)S(1)}, f32[4,256,256]{2,1,0:T(8,128)S(1)}, u32[]{:S(2)}, u32[]{:S(2)}) %collective-permute-start.2) | collective-permute-done | bytes 1048608 | tf_op jit(solution)/shard_map/ppermute | solution.py:152
  55.9 1.1 %add_bitcast_fusion = f32[4,1,256,256]{3,2,1,0:T(8,128)} fusion(f32[4,256,256]{2,1,0:T(8,128)S(1)} %get-tuple-element.35, f32[4,256,256]{2,1,0:T(8,128)S(1)} %collective-permute-done.2), kind=kLoop, calls=%fused_computation | loop fusion | flops 262144 | bytes 3145728 | tf_op jit(solution)/shard_map/reshape | solution.py:199
  (8 shorter events, 0.1 us)
Async XLA Ops:
  0.0 0.7 %copy-start.6 = (f32[1,1,256]{2,1,0:T(1,128)S(1)}, f32[1,1,256]{2,1,0:T(1,128)}, u32[]{:S(2)}) copy-start(f32[1,1,256]{2,1,0:T(1,128)} %param.17) | copy-start | bytes 3076
  0.0 0.7 %copy-start.5 = (s32[1,1,256]{2,1,0:T(1,128)S(1)}, s32[1,1,256]{2,1,0:T(1,128)}, u32[]{:S(2)}) copy-start(s32[1,1,256]{2,1,0:T(1,128)} %param.16) | copy-start | bytes 3076
  0.7 1.2 %copy-start = (f32[4,1,256,256]{3,2,1,0:T(8,128)S(1)}, f32[4,1,256,256]{3,2,1,0:T(8,128)}, u32[]{:S(2)}) copy-start(f32[4,1,256,256]{3,2,1,0:T(8,128)} %param.13) | copy-start | bytes 3145732
  1.9 0.9 %copy-start.3 = (s32[1,256,256]{2,1,0:T(8,128)S(1)}, s32[1,256,256]{2,1,0:T(8,128)}, u32[]{:S(2)}) copy-start(s32[1,256,256]{2,1,0:T(8,128)} %param.14) | copy-start | bytes 786436
  2.9 0.9 %copy-start.4 = (f32[1,256,256]{2,1,0:T(8,128)S(1)}, f32[1,256,256]{2,1,0:T(8,128)}, u32[]{:S(2)}) copy-start(f32[1,256,256]{2,1,0:T(8,128)} %param.15) | copy-start | bytes 786436
  15.8 6.3 %collective-permute-start = (f32[4,32,256]{2,1,0:T(8,128)S(1)}, f32[4,32,256]{2,1,0:T(8,128)S(1)}, u32[]{:S(2)}, u32[]{:S(2)}) collective-permute-start(f32[4,32,256]{2,1,0:T(8,128)S(1)} %get-tuple-element.38), channel_id=1, source_target_pairs={{0,1},{1,2},{2,3},{4,5},{5,6},{6,7},{8,9},{9,10},{10,11},{12,13},{... | collective-permute-start | bytes 393224 | tf_op jit(solution)/shard_map/ppermute | solution.py:152
  19.9 1.3 %copy-start.7 = (s32[1,256,1]{1,2,0:T(1,128)S(1)}, s32[1,256,1]{1,2,0:T(1,128)}, u32[]{:S(2)}) copy-start(s32[1,256,1]{1,2,0:T(1,128)} %param.20) | copy-start | bytes 3076
  19.9 5.7 %collective-permute-start.1 = (f32[4,32,256]{2,1,0:T(8,128)S(1)}, f32[4,32,256]{2,1,0:T(8,128)S(1)}, u32[]{:S(2)}, u32[]{:S(2)}) collective-permute-start(f32[4,32,256]{2,1,0:T(8,128)S(1)} %get-tuple-element.37), channel_id=1, source_target_pairs={{1,0},{2,1},{3,2},{5,4},{6,5},{7,6},{9,8},{10,9},{11,10},{13,12},{... | collective-permute-start | bytes 393224 | tf_op jit(solution)/shard_map/ppermute | solution.py:152
  21.3 0.7 %copy-start.8 = (f32[1,256,1]{1,2,0:T(1,128)S(1)}, f32[1,256,1]{1,2,0:T(1,128)}, u32[]{:S(2)}) copy-start(f32[1,256,1]{1,2,0:T(1,128)} %param.21) | copy-start | bytes 3076
  22.2 3.5 %copy-start.2 = (f32[1,256,256]{2,1,0:T(8,128)S(1)}, f32[1,256,256]{2,1,0:T(8,128)}, u32[]{:S(2)}) copy-start(f32[1,256,256]{2,1,0:T(8,128)} %param.19) | copy-start | bytes 786436
  22.2 3.4 %copy-start.1 = (s32[1,256,256]{2,1,0:T(8,128)S(1)}, s32[1,256,256]{2,1,0:T(8,128)}, u32[]{:S(2)}) copy-start(s32[1,256,256]{2,1,0:T(8,128)} %param.18) | copy-start | bytes 786436
  38.3 17.6 %collective-permute-start.2 = (f32[4,256,256]{2,1,0:T(8,128)S(1)}, f32[4,256,256]{2,1,0:T(8,128)S(1)}, u32[]{:S(2)}, u32[]{:S(2)}) collective-permute-start(f32[4,256,256]{2,1,0:T(8,128)S(1)} %get-tuple-element.36), channel_id=1, source_target_pairs={{4,0},{8,4},{12,8},{16,12},{20,16},{24,20},{28,24},{5,1},{9,5},{13... | collective-permute-start | bytes 3145736 | tf_op jit(solution)/shard_map/ppermute | solution.py:152
where the time goes:
time: 57.3 us; the launch traced here: 57 us
  Pallas kernels  24.6 us (43%)
  waiting for transfers between devices  16.9 us (29%)
  starting transfers between devices  9.34 us (16%)
  local copies, waits for them, and re-layouts  4.8 us (8%)
  other arithmetic  1.17 us (2%)
    ppermute x3, waiting for transfers between devices, passed_along(): return lax.ppermute(shard, axis, pairs)  16.9 us
    pallas_call x1, Pallas kernels, shards(): pl.pallas_call(lon_kernel, out_shape=(jax.ShapeDtypeStruct((tracers, rows...  12.7 us
    pallas_call x1, Pallas kernels, shards(): pl.pallas_call(lat_kernel, out_shape=(jax.ShapeDtypeStruct((tracers, rows...  12 us
    ppermute x3, starting transfers between devices, passed_along(): return lax.ppermute(shard, axis, pairs)  9.34 us
    unnamed x18, local copies, waits for them, and re-layouts  4.51 us
  transfers between devices with their start and end apart: 3, of which 2 were waited for; matrix products, arithmetic and copies ran while one was open for 1% of the time, Pallas kernels for 0%

commit v1 on v0

--- a/solution.py
+++ b/solution.py
@@ -9,6 +9,7 @@
 
 REACH = 32
 GROUP = 64
+SEND = 64
 
 
 def take(table, at):
@@ -74,9 +75,13 @@
     return now - jnp.where(lane == 0, before if before is None else pltpu.roll(before, 1, 1), pltpu.roll(now, 1, 1))
 
 
-def lat_kernel(cot_ref, cell_ref, frac_ref, endc_ref, endf_ref, own_ref, halo_ref, vt, et, endt, mt):
+MESH = pl.DeviceIdType.MESH
+
+
+def lat_pass(cot_ref, cell_ref, frac_ref, endc_ref, endf_ref, mid_ref, up_ref, down_ref, vt, et, endt, mt):
     tracers, lat_rows, cols = cot_ref.shape
     half = lat_rows // 2
+    reach = up_ref.shape[1]
     first_cell = lax.axis_index("lat") * lat_rows
     edges = (cell_ref[...] - first_cell).astype(jnp.float32) + frac_ref[...]
     et[...] = edges.T
@@ -109,97 +114,196 @@
                 mt[t, b, at, :] = step_up(got[b][t], got[b - 1][t])
 
     for t in range(tracers):
-        halo_ref[t] = mt[t, 0].T
-        own_ref[t, :half] = mt[t, 1].T
-        own_ref[t, half:] = mt[t, 2].T
-
-
-def lon_kernel(mid_ref, cell_ref, frac_ref, endc_ref, endf_ref, own_ref, low_ref):
+        halo = mt[t, 0].T
+        up_ref[t] = halo[:reach]
+        down_ref[t] = halo[half - reach :]
+
+
+def lon_group(at, first_cell, mid_ref, cell_ref, frac_ref, endc_ref, endf_ref, own_ref, low_ref, g, tri):
     tracers, rows, cols = mid_ref.shape
     half = cols // 2
-    first_cell = lax.axis_index("lon") * cols
+    group = low_ref.shape[2]
+    edges = (cell_ref[at, :] - first_cell).astype(jnp.float32) + frac_ref[at, :]
+    pair = (edges[:, :half], edges[:, half:])
+    last = (endc_ref[at, :] - first_cell).astype(jnp.float32) + endf_ref[at, :]
+    last = jnp.broadcast_to(last, (group, half))
+    values = [(mid_ref[t, at, :half], mid_ref[t, at, half:]) for t in range(tracers)]
+    sums = running(pair, last, values, tri)
+    lane = lanes_of(group, half)
+    halves = ((0,), (0, 1), (0, 1), (1,))
+    got = [
+        integral((lane + ((b - 2) * half + 1)).astype(jnp.float32), halves[b], pair, last, values, sums)
+        for b in range(4)
+    ]
+    none = jnp.zeros((group, half), jnp.float32)
+    for t in range(tracers):
+        for b in range(4):
+            cells = step_up(got[b][t], got[b - 1][t] if b else none)
+            start = (b % 2) * half
+            if b < 2:
+                low_ref[g, t, :, start : start + half] = cells
+            else:
+                own_ref[t, at, start : start + half] = cells
+
+
+def kernel(
+    lats, lons, cot_hbm, latc_hbm, latf_hbm, lat_endc, lat_endf, lonc_hbm, lonf_hbm, lon_endc, lon_endf,
+    out_ref, cot, latc, latf, lonc, lonf, vt, et, endt, mt, mid, edge_out, edge_in, low_out, low_in,
+    load_sem, edge_send, edge_recv, low_send, low_recv,
+):
+    tracers, rows, cols = cot.shape
+    half = rows // 2
+    reach = edge_out.shape[2]
+    groups, _, group, _ = low_out.shape
+    loads = [
+        pltpu.make_async_copy(source, target, load_sem.at[k])
+        for k, (source, target) in enumerate(
+            zip((latc_hbm, latf_hbm, cot_hbm, lonc_hbm, lonf_hbm), (latc, latf, cot, lonc, lonf))
+        )
+    ]
+    for load in loads:
+        load.start()
+    la, lo = lax.axis_index("lat"), lax.axis_index("lon")
+    has_up, has_down = la < lats - 1, la > 0
+    has_right, has_left = lo < lons - 1, lo > 0
+    barrier = pltpu.get_barrier_semaphore()
+    for there, where in (
+        (has_up, {"lat": la + 1}),
+        (has_down, {"lat": la - 1}),
+        (has_right, {"lon": lo + 1}),
+        (has_left, {"lon": lo - 1}),
+    ):
+
+        @pl.when(there)
+        def _(where=where):
+            pl.semaphore_signal(barrier, inc=1, device_id=where, device_id_type=MESH)
+
+    for load in loads:
+        load.wait()
+    lat_pass(cot, latc, latf, lat_endc, lat_endf, mid, edge_out.at[0], edge_out.at[1], vt, et, endt, mt)
+    peers = [there.astype(jnp.int32) for there in (has_up, has_down, has_right, has_left)]
+    pl.semaphore_wait(barrier, peers[0] + peers[1] + peers[2] + peers[3])
+
+    def edge(k, where):
+        return pltpu.make_async_remote_copy(
+            src_ref=edge_out.at[k],
+            dst_ref=edge_in.at[k],
+            send_sem=edge_send.at[k],
+            recv_sem=edge_recv.at[k],
+            device_id={"lat": where},
+            device_id_type=MESH,
+        )
+
+    up, down = edge(0, la + 1), edge(1, la - 1)
+    pl.when(has_up)(up.start)
+    pl.when(has_down)(down.start)
+    for t in range(tracers):
+        mid[t, :half] = mt[t, 1].T
+        mid[t, half:] = mt[t, 2].T
+
+    def low(g):
+        return pltpu.make_async_remote_copy(
+            src_ref=low_out.at[g],
+            dst_ref=low_in.at[g],
+            send_sem=low_send.at[g],
+            recv_sem=low_recv.at[g],
+            device_id={"lon": lo - 1},
+            device_id_type=MESH,
+        )
+
     tri = upper(cols)
-    group = min(GROUP, rows)
-
-    @pl.loop(0, rows // group)
-    def _(g):
+
+    @pl.loop(0, groups)
+    def _(k):
+        @pl.when(k == max(groups - 2, 0))
+        def _():
+            @pl.when(has_down)
+            def _():
+                up.wait_recv()
+                mid[:, :reach] += edge_in[0]
+
+            @pl.when(has_up)
+            def _():
+                down.wait_recv()
+                mid[:, rows - reach :] += edge_in[1]
+
+        g = lax.rem(k + 1, groups)
         at = pl.ds(pl.multiple_of(g * group, group), group)
-        edges = (cell_ref[at, :] - first_cell).astype(jnp.float32) + frac_ref[at, :]
-        pair = (edges[:, :half], edges[:, half:])
-        last = (endc_ref[at, :] - first_cell).astype(jnp.float32) + endf_ref[at, :]
-        last = jnp.broadcast_to(last, (group, half))
-        values = [(mid_ref[t, at, :half], mid_ref[t, at, half:]) for t in range(tracers)]
-        sums = running(pair, last, values, tri)
-        lane = lanes_of(group, half)
-        halves = ((0,), (0, 1), (0, 1), (1,))
-        got = [
-            integral((lane + ((b - 2) * half + 1)).astype(jnp.float32), halves[b], pair, last, values, sums)
-            for b in range(4)
-        ]
-        none = jnp.zeros((group, half), jnp.float32)
-        for t in range(tracers):
-            for b in range(4):
-                target = low_ref if b < 2 else own_ref
-                start = (b % 2) * half
-                target[t, at, start : start + half] = step_up(
-                    got[b][t], got[b - 1][t] if b else none
-                )
-
-
-def passed_along(shard, axis, by):
-    count = lax.axis_size(axis)
-    pairs = [(i, i + by) for i in range(count) if 0 <= i + by < count]
-    return lax.ppermute(shard, axis, pairs)
-
-
-def shards(cotangent, lat_cell, lat_frac, lat_end_cell, lat_end_frac, lon_cell, lon_frac, lon_end_cell, lon_end_frac):
+        lon_group(at, lo * cols, mid, lonc, lonf, lon_endc, lon_endf, out_ref, low_out, g, tri)
+        pl.when(has_left)(low(g).start)
+
+    @pl.when(has_right)
+    def _():
+        @pl.loop(0, groups)
+        def _(k):
+            g = lax.rem(k + 1, groups)
+            low(g).wait_recv()
+            at = pl.ds(pl.multiple_of(g * group, group), group)
+            out_ref[:, at, :] += low_in[g]
+
+    pl.when(has_up)(up.wait_send)
+    pl.when(has_down)(down.wait_send)
+
+    @pl.when(has_left)
+    def _():
+        @pl.loop(0, groups)
+        def _(g):
+            low(g).wait_send()
+
+
+def shards(lats, lons, cotangent, lat_cell, lat_frac, lat_end_cell, lat_end_frac, lon_cell, lon_frac, lon_end_cell, lon_end_frac):
     tracers, levels, rows, cols = cotangent.shape
-    f32 = jnp.float32
+    f32, i32 = jnp.float32, jnp.int32
     half = rows // 2
-    own, halo = pl.pallas_call(
-        lat_kernel,
-        out_shape=(
-            jax.ShapeDtypeStruct((tracers, rows, cols), f32),
-            jax.ShapeDtypeStruct((tracers, half, cols), f32),
-        ),
+    group = min(SEND, rows)
+    groups = rows // group
+    anywhere, vmem = pl.BlockSpec(memory_space=pl.ANY), pl.BlockSpec(memory_space=pltpu.VMEM)
+    out = pl.pallas_call(
+        functools.partial(kernel, lats, lons),
+        out_shape=jax.ShapeDtypeStruct((tracers, rows, cols), f32),
+        in_specs=[anywhere, anywhere, anywhere, vmem, vmem, anywhere, anywhere, vmem, vmem],
+        out_specs=vmem,
         scratch_shapes=[
+            pltpu.VMEM((tracers, rows, cols), f32),
+            pltpu.VMEM((rows, cols), i32),
+            pltpu.VMEM((rows, cols), f32),
+            pltpu.VMEM((rows, cols), i32),
+            pltpu.VMEM((rows, cols), f32),
             pltpu.VMEM((tracers, cols, rows), f32),
             pltpu.VMEM((cols, rows), f32),
             pltpu.VMEM((cols, half), f32),
             pltpu.VMEM((tracers, 3, cols, half), f32),
+            pltpu.VMEM((tracers, rows, cols), f32),
+            pltpu.VMEM((2, tracers, REACH, cols), f32),
+            pltpu.VMEM((2, tracers, REACH, cols), f32),
+            pltpu.VMEM((groups, tracers, group, cols), f32),
+            pltpu.VMEM((groups, tracers, group, cols), f32),
+            pltpu.SemaphoreType.DMA((5,)),
+            pltpu.SemaphoreType.DMA((2,)),
+            pltpu.SemaphoreType.DMA((2,)),
+            pltpu.SemaphoreType.DMA((groups,)),
+            pltpu.SemaphoreType.DMA((groups,)),
         ],
-        compiler_params=pltpu.CompilerParams(vmem_limit_bytes=48 * 2**20),
-        name="lat_pass",
+        compiler_params=pltpu.CompilerParams(
+            collective_id=0, has_side_effects=True, vmem_limit_bytes=48 * 2**20
+        ),
+        name="remap_adjoint",
     )(
         cotangent.reshape(tracers, rows, cols),
         lat_cell.reshape(rows, cols),
         lat_frac.reshape(rows, cols),
         lat_end_cell.reshape(1, cols),
         lat_end_frac.reshape(1, cols),
-    )
-    from_low = passed_along(halo[:, :REACH], "lat", 1)
-    from_high = passed_along(halo[:, half - REACH :], "lat", -1)
-    middle = own.at[:, :REACH].add(from_low).at[:, rows - REACH :].add(from_high)
-    own_part, low_part = pl.pallas_call(
-        lon_kernel,
-        out_shape=(
-            jax.ShapeDtypeStruct((tracers, rows, cols), f32),
-            jax.ShapeDtypeStruct((tracers, rows, cols), f32),
-        ),
-        compiler_params=pltpu.CompilerParams(vmem_limit_bytes=48 * 2**20),
-        name="lon_pass",
-    )(
-        middle,
         lon_cell.reshape(rows, cols),
         lon_frac.reshape(rows, cols),
         lon_end_cell.reshape(rows, 1),
         lon_end_frac.reshape(rows, 1),
     )
-    out = own_part + passed_along(low_part, "lon", -1)
     return out.reshape(cotangent.shape)
 
 
 def solution(mesh):
     whole = P(None, None, "lat", "lon")
     placed = (whole,) + (P(None, "lat", "lon"),) * 8
-    return jax.shard_map(shards, mesh=mesh, in_specs=placed, out_specs=whole, check_vma=False)
+    body = functools.partial(shards, mesh.shape["lat"], mesh.shape["lon"])
+    return jax.shard_map(body, mesh=mesh, in_specs=placed, out_specs=whole, check_vma=False)

time: 57.3 us -> 38.8 us (0.68)
  waiting for transfers between devices: 16.9 us -> 0 us
  starting transfers between devices: 9.34 us -> 0 us
  Pallas kernels: 24.6 us -> 31.8 us
  local copies, waits for them, and re-layouts: 4.8 us -> 6.72 us
  other arithmetic: 1.17 us -> 0 us
    ppermute x3 -> x0, waiting for transfers between devices: 16.9 us -> none  [passed_along(): return lax.ppermute(shard, axis, pairs)]
    ppermute x3 -> x0, starting transfers between devices: 9.34 us -> none  [passed_along(): return lax.ppermute(shard, axis, pairs)]
    pallas_call x2 -> x1, Pallas kernels: 24.6 us -> 31.8 us  [shards(): pl.pallas_call(functools.partial(kernel, lats, lons), out_shape=jax.Shape...]
    reshape x1 -> x0, other arithmetic: 1.1 us -> none  [shards(): return out.reshape(cotangent.shape)]
    reshape x1, local copies, waits for them, and re-layouts: 0.13 us -> 0.85 us  [shards(): lon_end_cell.reshape(rows, 1)]
    reshape x1, local copies, waits for them, and re-layouts: 0.13 us -> 0.82 us  [shards(): lon_end_frac.reshape(rows, 1)]
    unnamed x18 -> x15, local copies, waits for them, and re-layouts: 4.51 us -> 5.06 us
  transfers between devices with their start and end apart: 3 -> 0, of which waited for: 2 -> 0; matrix products, arithmetic and copies ran while one was open for 1% -> 0% of each run, Pallas kernels for 0% -> 0%
where the time goes in v1:
time: 38.8 us; the launch traced here: 38.6 us
  Pallas kernels  31.8 us (82%)
  local copies, waits for them, and re-layouts  6.72 us (17%)
    pallas_call x1, Pallas kernels, shards(): pl.pallas_call(functools.partial(kernel, lats, lons), out_shape=jax.Shape...  31.8 us
    unnamed x15, local copies, waits for them, and re-layouts  5.06 us
    reshape x1, local copies, waits for them, and re-layouts, shards(): lon_end_cell.reshape(rows, 1)  0.85 us
    reshape x1, local copies, waits for them, and re-layouts, shards(): lon_end_frac.reshape(rows, 1)  0.82 us

profile of v1, /device:TPU:1, one launch (start us, length us, event | category | flops | bytes accessed | tf_op | source)
XLA Modules:
  0.0 38.6 jit_solution(14234317013475717596)
XLA Ops:
  0.0 0.0 copy-start.1
  0.0 0.8 %copy.11.lon_endc = s32[256,1]{1,0:T(8,128)S(1)} copy(s32[256,1]{0,1:T(1,128)} %bitcast.20) | data formatting | bytes 2048 | tf_op jit(solution)/shard_map/reshape | solution.py:299
  0.9 0.0 copy-start.5
  0.9 0.0 copy-start.6
  0.9 0.8 %copy.12.lon_endf = f32[256,1]{1,0:T(8,128)S(1)} copy(f32[256,1]{0,1:T(1,128)} %bitcast.21) | data formatting | bytes 2048 | tf_op jit(solution)/shard_map/reshape | solution.py:300
  1.7 0.0 copy-done.1
  1.7 0.0 copy-done.5
  1.7 0.0 copy-done.6
  1.7 0.0 copy-start
  1.8 1.2 %copy-done = f32[4,1,256,256]{3,2,1,0:T(8,128)S(1)} copy-done((f32[4,1,256,256]{3,2,1,0:T(8,128)S(1)}, f32[4,1,256,256]{3,2,1,0:T(8,128)}, u32[]{:S(2)}) %copy-start) | copy-done | bytes 1048600
  3.0 0.0 copy-start.2
  3.0 0.9 %copy-done.2 = f32[1,256,256]{2,1,0:T(8,128)S(1)} copy-done((f32[1,256,256]{2,1,0:T(8,128)S(1)}, f32[1,256,256]{2,1,0:T(8,128)}, u32[]{:S(2)}) %copy-start.2) | copy-done | bytes 262168
  3.9 0.0 copy-start.3
  3.9 0.9 %copy-done.3 = s32[1,256,256]{2,1,0:T(8,128)S(1)} copy-done((s32[1,256,256]{2,1,0:T(8,128)S(1)}, s32[1,256,256]{2,1,0:T(8,128)}, u32[]{:S(2)}) %copy-start.3) | copy-done | bytes 262168
  4.9 0.0 copy-start.4
  4.9 0.9 %copy-done.4 = f32[1,256,256]{2,1,0:T(8,128)S(1)} copy-done((f32[1,256,256]{2,1,0:T(8,128)S(1)}, f32[1,256,256]{2,1,0:T(8,128)}, u32[]{:S(2)}) %copy-start.4) | copy-done | bytes 262168
  5.8 31.8 %remap_adjoint.1 = f32[4,256,256]{2,1,0:T(8,128)S(1)} custom-call(f32[4,256,256]{2,1,0:T(8,128)S(1)} %bitcast.13, s32[256,256]{1,0:T(8,128)S(1)} %bitcast.14, f32[256,256]{1,0:T(8,128)S(1)} %bitcast.15, s32[1,256]{1,0:T(1,128)S(1)} %bitcast.18, f32[1,256]{1,0:T(1,128)S(1)} %bitcast.19, s32[256,256]{1,0:T(8,128)S(1)} %bitcast.16, f32[256,256]{1,0:T(8,128)S(1)} %bitcast.17, ...), custom_call_target="tpu_custom_call" | custom-call | tf_op jit(solution)/shard_map/remap_adjoint/pallas_call | solution.py:261
  37.6 1.0 %copy.15 = f32[4,1,256,256]{3,2,1,0:T(8,128)} copy(f32[4,1,256,256]{3,2,1,0:T(8,128)S(1)} %bitcast.12) | data formatting | bytes 2097152
Async XLA Ops:
  0.0 1.7 %copy-start.1 = (s32[1,256,256]{2,1,0:T(8,128)S(1)}, s32[1,256,256]{2,1,0:T(8,128)}, u32[]{:S(2)}) copy-start(s32[1,256,256]{2,1,0:T(8,128)} %param.10) | copy-start | bytes 786436
  0.9 0.9 %copy-start.5 = (s32[1,1,256]{2,1,0:T(1,128)S(1)}, s32[1,1,256]{2,1,0:T(1,128)}, u32[]{:S(2)}) copy-start(s32[1,1,256]{2,1,0:T(1,128)} %param.12) | copy-start | bytes 3076
  0.9 0.9 %copy-start.6 = (f32[1,1,256]{2,1,0:T(1,128)S(1)}, f32[1,1,256]{2,1,0:T(1,128)}, u32[]{:S(2)}) copy-start(f32[1,1,256]{2,1,0:T(1,128)} %param.13) | copy-start | bytes 3076
  1.7 1.2 %copy-start = (f32[4,1,256,256]{3,2,1,0:T(8,128)S(1)}, f32[4,1,256,256]{3,2,1,0:T(8,128)}, u32[]{:S(2)}) copy-start(f32[4,1,256,256]{3,2,1,0:T(8,128)} %param.9) | copy-start | bytes 3145732
  3.0 0.9 %copy-start.2 = (f32[1,256,256]{2,1,0:T(8,128)S(1)}, f32[1,256,256]{2,1,0:T(8,128)}, u32[]{:S(2)}) copy-start(f32[1,256,256]{2,1,0:T(8,128)} %param.11) | copy-start | bytes 786436
  3.9 0.9 %copy-start.3 = (s32[1,256,256]{2,1,0:T(8,128)S(1)}, s32[1,256,256]{2,1,0:T(8,128)}, u32[]{:S(2)}) copy-start(s32[1,256,256]{2,1,0:T(8,128)} %param.14) | copy-start | bytes 786436
  4.9 0.9 %copy-start.4 = (f32[1,256,256]{2,1,0:T(8,128)S(1)}, f32[1,256,256]{2,1,0:T(8,128)}, u32[]{:S(2)}) copy-start(f32[1,256,256]{2,1,0:T(8,128)} %param.15) | copy-start | bytes 786436

commit v2 on v1

--- a/solution.py
+++ b/solution.py
@@ -8,8 +8,9 @@
 from jax.sharding import PartitionSpec as P
 
 REACH = 32
-GROUP = 64
-SEND = 64
+GROUP = 128
+SEND = 32
+VMEM = 63 * 2**20
 
 
 def take(table, at):
@@ -39,35 +40,71 @@
     )
     high = whole.astype(jnp.bfloat16)
     low = (whole - high.astype(jnp.float32)).astype(jnp.bfloat16)
-    total = jnp.dot(high, tri, preferred_element_type=jnp.float32) + jnp.dot(
-        low, tri, preferred_element_type=jnp.float32
-    )
+    both = jnp.dot(jnp.concatenate([high, low], axis=0), tri, preferred_element_type=jnp.float32)
+    count = whole.shape[0]
+    total = both[:count] + both[count:]
     return [
-        (total[t * rows : (t + 1) * rows, :half], total[t * rows : (t + 1) * rows, half:])
+        tuple(
+            total[t * rows : (t + 1) * rows, h * half : (h + 1) * half] - values[t][h] * edges[h]
+            for h in (0, 1)
+        )
         for t in range(len(values))
     ]
 
 
-def integral(points, halves, edges, end, values, sums):
-    rows, half = edges[0].shape
-    first = jnp.broadcast_to(edges[0][:, :1], (rows, half))
-    x = jnp.minimum(jnp.maximum(points, first), end)
+def spread(table, lane, shape):
+    return jnp.broadcast_to(table[:, lane : lane + 1], shape)
+
+
+def integral(points, halves, edges, marks, end, values, starts):
+    shape = edges[0].shape
+    half = shape[1]
+    x = jnp.minimum(jnp.maximum(points, marks[0][0]), end)
     if len(halves) == 2:
-        upper_half = jnp.broadcast_to(edges[1][:, :1], (rows, half)) <= x
+        upper_half = marks[1][0] <= x
+
+    def pick(pair):
+        if len(halves) == 1:
+            return pair[halves[0]]
+        return jnp.where(upper_half, pair[1], pair[0])
 
     def fetch(pair, at):
         if len(halves) == 1:
             return take(pair[halves[0]], at)
         return jnp.where(upper_half, take(pair[1], at), take(pair[0], at))
 
-    at = jnp.zeros((rows, half), jnp.int32)
     step = half // 2
+    at = jnp.where(pick((marks[0][1], marks[1][1])) <= x, step, 0)
+    step //= 2
     while step:
         further = at + step
         at = jnp.where(fetch(edges, further) <= x, further, at)
         step //= 2
-    inside = x - fetch(edges, at)
-    return [fetch(s, at) + fetch(v, at) * inside for s, v in zip(sums, values)]
+    return [fetch(s, at) + fetch(v, at) * x for s, v in zip(starts, values)]
+
+
+def near_integral(points, reach, source, edges, first, end, values, starts):
+    half = edges[0].shape[1]
+    length = 2 * half
+    x = jnp.minimum(jnp.maximum(points.astype(jnp.float32), first), end)
+
+    def fetch(pair, at):
+        lane = jnp.bitwise_and(at, half - 1)
+        if source is not None:
+            return take(pair, lane)
+        return jnp.where(at >= half, take(pair[1], lane), take(pair[0], lane))
+
+    at = points - reach
+    step = reach
+    while step:
+        further = at + step
+        found = fetch(edges if source is None else source[0], further)
+        ahead = jnp.logical_and(further < length, jnp.logical_or(further < 0, found <= x))
+        at = jnp.where(ahead, further, at)
+        step //= 2
+    at = jnp.clip(at, 0, length - 1)
+    tables = zip(starts, values) if source is None else zip(source[1], source[2])
+    return [fetch(s, at) + fetch(v, at) * x for s, v in tables]
 
 
 def step_up(now, before):
@@ -100,14 +137,16 @@
         values = [(vt[t, at, :half], vt[t, at, half:]) for t in range(tracers)]
         sums = running(pair, last, values, tri)
         lane = lanes_of(group, half)
-        places = (
-            jnp.where(lane < half // 2, lane + 2 * half, lane - half),
-            lane,
-            lane + half,
-        )
+        first = spread(pair[0], 0, pair[0].shape)
+        rim = jnp.where(lane < half // 2, lane + 2 * half, lane - half)
+
+        def ends(both):
+            return jnp.where(lane < half // 2, both[0], both[1])
+
+        source = (ends(pair), [ends(s) for s in sums], [ends(v) for v in values])
         got = [
-            integral((p + 1).astype(jnp.float32), (0, 1), pair, last, values, sums)
-            for p in places
+            near_integral(p + 1, reach, src, pair, first, last, values, sums)
+            for p, src in ((rim, source), (lane, None), (lane + half, None))
         ]
         for t in range(tracers):
             for b in range(3):
@@ -119,20 +158,20 @@
         down_ref[t] = halo[half - reach :]
 
 
-def lon_group(at, first_cell, mid_ref, cell_ref, frac_ref, endc_ref, endf_ref, own_ref, low_ref, g, tri):
+def lon_group(at, first_cell, mid_ref, cell_ref, frac_ref, end_ref, own_ref, low_ref, g, tri):
     tracers, rows, cols = mid_ref.shape
     half = cols // 2
     group = low_ref.shape[2]
     edges = (cell_ref[at, :] - first_cell).astype(jnp.float32) + frac_ref[at, :]
     pair = (edges[:, :half], edges[:, half:])
-    last = (endc_ref[at, :] - first_cell).astype(jnp.float32) + endf_ref[at, :]
-    last = jnp.broadcast_to(last, (group, half))
+    last = end_ref[at, :]
     values = [(mid_ref[t, at, :half], mid_ref[t, at, half:]) for t in range(tracers)]
     sums = running(pair, last, values, tri)
     lane = lanes_of(group, half)
     halves = ((0,), (0, 1), (0, 1), (1,))
+    marks = [[spread(edge, at, edge.shape) for at in (0, half // 2)] for edge in pair]
     got = [
-        integral((lane + ((b - 2) * half + 1)).astype(jnp.float32), halves[b], pair, last, values, sums)
+        integral((lane + ((b - 2) * half + 1)).astype(jnp.float32), halves[b], pair, marks, last, values, sums)
         for b in range(4)
     ]
     none = jnp.zeros((group, half), jnp.float32)
@@ -148,7 +187,7 @@
 
 def kernel(
     lats, lons, cot_hbm, latc_hbm, latf_hbm, lat_endc, lat_endf, lonc_hbm, lonf_hbm, lon_endc, lon_endf,
-    out_ref, cot, latc, latf, lonc, lonf, vt, et, endt, mt, mid, edge_out, edge_in, low_out, low_in,
+    out_ref, cot, latc, latf, lonc, lonf, vt, et, endt, mt, mid, lon_end, edge_out, edge_in, low_out, low_in,
     load_sem, edge_send, edge_recv, low_send, low_recv,
 ):
     tracers, rows, cols = cot.shape
@@ -178,6 +217,8 @@
         def _(where=where):
             pl.semaphore_signal(barrier, inc=1, device_id=where, device_id_type=MESH)
 
+    end = (lon_endc[...] - lo * cols).astype(jnp.float32) + lon_endf[...]
+    lon_end[...] = jnp.broadcast_to(end, (cols // 2, rows)).T
     for load in loads:
         load.wait()
     lat_pass(cot, latc, latf, lat_endc, lat_endf, mid, edge_out.at[0], edge_out.at[1], vt, et, endt, mt)
@@ -229,7 +270,7 @@
 
         g = lax.rem(k + 1, groups)
         at = pl.ds(pl.multiple_of(g * group, group), group)
-        lon_group(at, lo * cols, mid, lonc, lonf, lon_endc, lon_endf, out_ref, low_out, g, tri)
+        lon_group(at, lo * cols, mid, lonc, lonf, lon_end, out_ref, low_out, g, tri)
         pl.when(has_left)(low(g).start)
 
     @pl.when(has_right)
@@ -274,6 +315,7 @@
             pltpu.VMEM((cols, half), f32),
             pltpu.VMEM((tracers, 3, cols, half), f32),
             pltpu.VMEM((tracers, rows, cols), f32),
+            pltpu.VMEM((rows, cols // 2), f32),
             pltpu.VMEM((2, tracers, REACH, cols), f32),
             pltpu.VMEM((2, tracers, REACH, cols), f32),
             pltpu.VMEM((groups, tracers, group, cols), f32),
@@ -285,7 +327,7 @@
             pltpu.SemaphoreType.DMA((groups,)),
         ],
         compiler_params=pltpu.CompilerParams(
-            collective_id=0, has_side_effects=True, vmem_limit_bytes=48 * 2**20
+            collective_id=0, has_side_effects=True, vmem_limit_bytes=VMEM
         ),
         name="remap_adjoint",
     )(
@@ -296,8 +338,8 @@
         lat_end_frac.reshape(1, cols),
         lon_cell.reshape(rows, cols),
         lon_frac.reshape(rows, cols),
-        lon_end_cell.reshape(rows, 1),
-        lon_end_frac.reshape(rows, 1),
+        lon_end_cell.reshape(1, rows),
+        lon_end_frac.reshape(1, rows),
     )
     return out.reshape(cotangent.shape)
 

time: 38.8 us -> 31.2 us (0.80)
  local copies, waits for them, and re-layouts: 6.72 us -> 2.29 us
  Pallas kernels: 31.8 us -> 28.7 us
    pallas_call x1, Pallas kernels: 31.8 us -> 28.7 us  [shards(): pl.pallas_call(functools.partial(kernel, lats, lons), out_shape=jax.Shape...]
    unnamed x15 -> x1, local copies, waits for them, and re-layouts: 5.06 us -> 2.29 us
    reshape x2 -> x0, local copies, waits for them, and re-layouts: 1.67 us -> none  [the longest x1 0.85 us: shards(): lon_end_cell.reshape(rows, 1)]
where the time goes in v2:
time: 31.2 us; the launch traced here: 31 us
  Pallas kernels  28.7 us (92%)
  local copies, waits for them, and re-layouts  2.29 us (7%)
    pallas_call x1, Pallas kernels, shards(): pl.pallas_call(functools.partial(kernel, lats, lons), out_shape=jax.Shape...  28.7 us
    unnamed x1, local copies, waits for them, and re-layouts  2.29 us

profile of v2, /device:TPU:1, one launch (start us, length us, event | category | flops | bytes accessed | tf_op | source)
XLA Modules:
  0.0 31.0 jit_solution(5698087049175317324)
XLA Ops:
  0.0 28.7 %remap_adjoint.1 = f32[4,256,256]{2,1,0:T(8,128)} custom-call(f32[4,256,256]{2,1,0:T(8,128)} %bitcast.13, s32[256,256]{1,0:T(8,128)} %bitcast.14, f32[256,256]{1,0:T(8,128)} %bitcast.15, s32[1,256]{1,0:T(1,128)} %bitcast.18, f32[1,256]{1,0:T(1,128)} %bitcast.19, s32[256,256]{1,0:T(8,128)} %bitcast.16, f32[256,256]{1,0:T(8,128)} %bitcast.17, ...), custom_call_target="tpu_custom_call" | custom-call | tf_op jit(solution)/shard_map/remap_adjoint/pallas_call | solution.py:302
  28.7 2.3 %copy.12 = f32[4,1,256,256]{3,2,1,0:T(8,128)} copy(f32[4,1,256,256]{3,2,1,0:T(8,128)} %bitcast.12) | data formatting | bytes 2097152

commit v3 on v2

--- a/solution.py
+++ b/solution.py
@@ -115,7 +115,7 @@
 MESH = pl.DeviceIdType.MESH
 
 
-def lat_pass(cot_ref, cell_ref, frac_ref, endc_ref, endf_ref, mid_ref, up_ref, down_ref, vt, et, endt, mt):
+def lat_first(cot_ref, cell_ref, frac_ref, endc_ref, endf_ref, up_ref, down_ref, vt, st, et, endt, mt):
     tracers, lat_rows, cols = cot_ref.shape
     half = lat_rows // 2
     reach = up_ref.shape[1]
@@ -138,24 +138,47 @@
         sums = running(pair, last, values, tri)
         lane = lanes_of(group, half)
         first = spread(pair[0], 0, pair[0].shape)
-        rim = jnp.where(lane < half // 2, lane + 2 * half, lane - half)
+        rim = jnp.where(lane < half // 2, lane + 2 * half, lane - half + 1)
 
         def ends(both):
             return jnp.where(lane < half // 2, both[0], both[1])
 
         source = (ends(pair), [ends(s) for s in sums], [ends(v) for v in values])
         got = [
-            near_integral(p + 1, reach, src, pair, first, last, values, sums)
-            for p, src in ((rim, source), (lane, None), (lane + half, None))
+            near_integral(p, reach, src, pair, first, last, values, sums)
+            for p, src in ((rim, source), (lane + 1, None))
         ]
         for t in range(tracers):
-            for b in range(3):
-                mt[t, b, at, :] = step_up(got[b][t], got[b - 1][t])
+            st[t, at, :half], st[t, at, half:] = sums[t]
+            mt[t, 0, at, :] = step_up(got[0][t], got[0][t])
+            mt[t, 1, at, :] = step_up(got[1][t], got[0][t])
+            mt[t, 2, at, :] = got[1][t]
 
     for t in range(tracers):
         halo = mt[t, 0].T
-        up_ref[t] = halo[:reach]
+        up_ref[t] = halo[1 : reach + 1]
         down_ref[t] = halo[half - reach :]
+
+
+def lat_second(reach, mid_ref, vt, st, et, endt, mt):
+    tracers, cols, lat_rows = vt.shape
+    half = lat_rows // 2
+    group = min(GROUP, cols)
+
+    @pl.loop(0, cols // group)
+    def _(g):
+        at = pl.ds(pl.multiple_of(g * group, group), group)
+        pair = (et[at, :half], et[at, half:])
+        values = [(vt[t, at, :half], vt[t, at, half:]) for t in range(tracers)]
+        starts = [(st[t, at, :half], st[t, at, half:]) for t in range(tracers)]
+        first = spread(pair[0], 0, pair[0].shape)
+        points = lanes_of(group, half) + (half + 1)
+        got = near_integral(points, reach, None, pair, first, endt[at, :], values, starts)
+        for t in range(tracers):
+            mt[t, 2, at, :] = step_up(got[t], mt[t, 2, at, :])
+
+    for t in range(tracers):
+        mid_ref[t, half:] = mt[t, 2].T
 
 
 def lon_group(at, first_cell, mid_ref, cell_ref, frac_ref, end_ref, own_ref, low_ref, g, tri):
@@ -187,7 +210,7 @@
 
 def kernel(
     lats, lons, cot_hbm, latc_hbm, latf_hbm, lat_endc, lat_endf, lonc_hbm, lonf_hbm, lon_endc, lon_endf,
-    out_ref, cot, latc, latf, lonc, lonf, vt, et, endt, mt, mid, lon_end, edge_out, edge_in, low_out, low_in,
+    out_ref, cot, latc, latf, lonc, lonf, vt, st, et, endt, mt, mid, lon_end, edge_out, edge_in, low_out, low_in,
     load_sem, edge_send, edge_recv, low_send, low_recv,
 ):
     tracers, rows, cols = cot.shape
@@ -221,7 +244,7 @@
     lon_end[...] = jnp.broadcast_to(end, (cols // 2, rows)).T
     for load in loads:
         load.wait()
-    lat_pass(cot, latc, latf, lat_endc, lat_endf, mid, edge_out.at[0], edge_out.at[1], vt, et, endt, mt)
+    lat_first(cot, latc, latf, lat_endc, lat_endf, edge_out.at[0], edge_out.at[1], vt, st, et, endt, mt)
     peers = [there.astype(jnp.int32) for there in (has_up, has_down, has_right, has_left)]
     pl.semaphore_wait(barrier, peers[0] + peers[1] + peers[2] + peers[3])
 
@@ -240,7 +263,6 @@
     pl.when(has_down)(down.start)
     for t in range(tracers):
         mid[t, :half] = mt[t, 1].T
-        mid[t, half:] = mt[t, 2].T
 
     def low(g):
         return pltpu.make_async_remote_copy(
@@ -256,6 +278,10 @@
 
     @pl.loop(0, groups)
     def _(k):
+        @pl.when(k == max(groups // 2 - 1, 0))
+        def _():
+            lat_second(reach, mid, vt, st, et, endt, mt)
+
         @pl.when(k == max(groups - 2, 0))
         def _():
             @pl.when(has_down)
@@ -310,6 +336,7 @@
             pltpu.VMEM((rows, cols), f32),
             pltpu.VMEM((rows, cols), i32),
             pltpu.VMEM((rows, cols), f32),
+            pltpu.VMEM((tracers, cols, rows), f32),
             pltpu.VMEM((tracers, cols, rows), f32),
             pltpu.VMEM((cols, rows), f32),
             pltpu.VMEM((cols, half), f32),

time: 31.2 us -> 31.2 us (level)
  no operation moved by 1% of the time
where the time goes in v3:
time: 31.2 us; the launch traced here: 31 us
  Pallas kernels  28.7 us (92%)
  local copies, waits for them, and re-layouts  2.29 us (7%)
    pallas_call x1, Pallas kernels, shards(): pl.pallas_call(functools.partial(kernel, lats, lons), out_shape=jax.Shape...  28.7 us
    unnamed x1, local copies, waits for them, and re-layouts  2.29 us

profile of v3, /device:TPU:1, one launch (start us, length us, event | category | flops | bytes accessed | tf_op | source)
XLA Modules:
  0.0 31.0 jit_solution(10032679667897134231)
XLA Ops:
  0.0 28.7 %remap_adjoint.1 = f32[4,256,256]{2,1,0:T(8,128)} custom-call(f32[4,256,256]{2,1,0:T(8,128)} %bitcast.13, s32[256,256]{1,0:T(8,128)} %bitcast.14, f32[256,256]{1,0:T(8,128)} %bitcast.15, s32[1,256]{1,0:T(1,128)} %bitcast.18, f32[1,256]{1,0:T(1,128)} %bitcast.19, s32[256,256]{1,0:T(8,128)} %bitcast.16, f32[256,256]{1,0:T(8,128)} %bitcast.17, ...), custom_call_target="tpu_custom_call" | custom-call | tf_op jit(solution)/shard_map/remap_adjoint/pallas_call | solution.py:328
  28.7 2.3 %copy.12 = f32[4,1,256,256]{3,2,1,0:T(8,128)} copy(f32[4,1,256,256]{3,2,1,0:T(8,128)} %bitcast.12) | data formatting | bytes 2097152

commit v4 on v3

--- a/solution.py
+++ b/solution.py
@@ -74,7 +74,10 @@
         return jnp.where(upper_half, take(pair[1], at), take(pair[0], at))
 
     step = half // 2
-    at = jnp.where(pick((marks[0][1], marks[1][1])) <= x, step, 0)
+    beyond = pick((marks[0][2], marks[1][2])) <= x
+    step //= 2
+    middle = pick([jnp.where(beyond, mark[3], mark[1]) for mark in marks])
+    at = jnp.where(beyond, 2 * step, 0) + jnp.where(middle <= x, step, 0)
     step //= 2
     while step:
         further = at + step
@@ -115,7 +118,7 @@
 MESH = pl.DeviceIdType.MESH
 
 
-def lat_first(cot_ref, cell_ref, frac_ref, endc_ref, endf_ref, up_ref, down_ref, vt, st, et, endt, mt):
+def lat_first(wait, cot_ref, cell_ref, frac_ref, endc_ref, endf_ref, up_ref, down_ref, vt, st, et, endt, mt):
     tracers, lat_rows, cols = cot_ref.shape
     half = lat_rows // 2
     reach = up_ref.shape[1]
@@ -124,6 +127,7 @@
     et[...] = edges.T
     end = (endc_ref[...] - first_cell).astype(jnp.float32) + endf_ref[...]
     endt[...] = jnp.broadcast_to(end, (half, cols)).T
+    wait()
     for t in range(tracers):
         vt[t] = cot_ref[t].T
     tri = upper(lat_rows)
@@ -192,7 +196,7 @@
     sums = running(pair, last, values, tri)
     lane = lanes_of(group, half)
     halves = ((0,), (0, 1), (0, 1), (1,))
-    marks = [[spread(edge, at, edge.shape) for at in (0, half // 2)] for edge in pair]
+    marks = [[spread(edge, at, edge.shape) for at in (0, half // 4, half // 2, 3 * (half // 4))] for edge in pair]
     got = [
         integral((lane + ((b - 2) * half + 1)).astype(jnp.float32), halves[b], pair, marks, last, values, sums)
         for b in range(4)
@@ -242,9 +246,9 @@
 
     end = (lon_endc[...] - lo * cols).astype(jnp.float32) + lon_endf[...]
     lon_end[...] = jnp.broadcast_to(end, (cols // 2, rows)).T
-    for load in loads:
-        load.wait()
-    lat_first(cot, latc, latf, lat_endc, lat_endf, edge_out.at[0], edge_out.at[1], vt, st, et, endt, mt)
+    loads[0].wait()
+    loads[1].wait()
+    lat_first(loads[2].wait, cot, latc, latf, lat_endc, lat_endf, edge_out.at[0], edge_out.at[1], vt, st, et, endt, mt)
     peers = [there.astype(jnp.int32) for there in (has_up, has_down, has_right, has_left)]
     pl.semaphore_wait(barrier, peers[0] + peers[1] + peers[2] + peers[3])
 
@@ -275,6 +279,8 @@
         )
 
     tri = upper(cols)
+    loads[3].wait()
+    loads[4].wait()
 
     @pl.loop(0, groups)
     def _(k):

time: 31.2 us -> 30.8 us (0.987)
  Pallas kernels: 28.7 us -> 28.3 us
    pallas_call x1, Pallas kernels: 28.7 us -> 28.3 us  [shards(): pl.pallas_call(functools.partial(kernel, lats, lons), out_shape=jax.Shape...]
where the time goes in v4:
time: 30.8 us; the launch traced here: 30.6 us
  Pallas kernels  28.3 us (92%)
  local copies, waits for them, and re-layouts  2.29 us (7%)
    pallas_call x1, Pallas kernels, shards(): pl.pallas_call(functools.partial(kernel, lats, lons), out_shape=jax.Shape...  28.3 us
    unnamed x1, local copies, waits for them, and re-layouts  2.29 us

profile of v4, /device:TPU:1, one launch (start us, length us, event | category | flops | bytes accessed | tf_op | source)
XLA Modules:
  0.0 30.6 jit_solution(550854229606386423)
XLA Ops:
  0.0 28.3 %remap_adjoint.1 = f32[4,256,256]{2,1,0:T(8,128)} custom-call(f32[4,256,256]{2,1,0:T(8,128)} %bitcast.13, s32[256,256]{1,0:T(8,128)} %bitcast.14, f32[256,256]{1,0:T(8,128)} %bitcast.15, s32[1,256]{1,0:T(1,128)} %bitcast.18, f32[1,256]{1,0:T(1,128)} %bitcast.19, s32[256,256]{1,0:T(8,128)} %bitcast.16, f32[256,256]{1,0:T(8,128)} %bitcast.17, ...), custom_call_target="tpu_custom_call" | custom-call | tf_op jit(solution)/shard_map/remap_adjoint/pallas_call | solution.py:334
  28.3 2.3 %copy.12 = f32[4,1,256,256]{3,2,1,0:T(8,128)} copy(f32[4,1,256,256]{3,2,1,0:T(8,128)} %bitcast.12) | data formatting | bytes 2097152

commit v5 on v4

--- a/solution.py
+++ b/solution.py
@@ -8,7 +8,7 @@
 from jax.sharding import PartitionSpec as P
 
 REACH = 32
-GROUP = 128
+GROUP = 256
 SEND = 32
 VMEM = 63 * 2**20
 

time: 30.8 us -> 29.5 us (0.958)
  Pallas kernels: 28.3 us -> 27 us
    pallas_call x1, Pallas kernels: 28.3 us -> 27 us  [shards(): pl.pallas_call(functools.partial(kernel, lats, lons), out_shape=jax.Shape...]
where the time goes in v5:
time: 29.5 us; the launch traced here: 29.3 us
  Pallas kernels  27 us (92%)
  local copies, waits for them, and re-layouts  2.29 us (8%)
    pallas_call x1, Pallas kernels, shards(): pl.pallas_call(functools.partial(kernel, lats, lons), out_shape=jax.Shape...  27 us
    unnamed x1, local copies, waits for them, and re-layouts  2.29 us

profile of v5, /device:TPU:1, one launch (start us, length us, event | category | flops | bytes accessed | tf_op | source)
XLA Modules:
  0.0 29.3 jit_solution(14845091409691463955)
XLA Ops:
  0.0 27.0 %remap_adjoint.1 = f32[4,256,256]{2,1,0:T(8,128)} custom-call(f32[4,256,256]{2,1,0:T(8,128)} %bitcast.13, s32[256,256]{1,0:T(8,128)} %bitcast.14, f32[256,256]{1,0:T(8,128)} %bitcast.15, s32[1,256]{1,0:T(1,128)} %bitcast.18, f32[1,256]{1,0:T(1,128)} %bitcast.19, s32[256,256]{1,0:T(8,128)} %bitcast.16, f32[256,256]{1,0:T(8,128)} %bitcast.17, ...), custom_call_target="tpu_custom_call" | custom-call | tf_op jit(solution)/shard_map/remap_adjoint/pallas_call | solution.py:334
  27.0 2.3 %copy.12 = f32[4,1,256,256]{3,2,1,0:T(8,128)} copy(f32[4,1,256,256]{3,2,1,0:T(8,128)} %bitcast.12) | data formatting | bytes 2097152
